TPU v7x, 128 devices: a whole 4x4x4 slice. The times are simulated.
128 devices in a mesh: band: 4 (over z_hi, core), dom: 32 (over y, z_lo, x).
Axes of the slice: x: 4, y: 4, z: 4 (z_hi: 2, z_lo: 2; z = z_hi * 2 + z_lo), core: 2. Of those that a mesh axis runs over, the one named last changes fastest.
Arguments:
- orbitals: bfloat16 [512, 128, 32, 256], P('band', 'dom'), may hold values from -0.1875 to 0.1875
- potential: float32 [128, 32, 256], P('dom'), may hold values from 0.5 to 2.5
- projectors: bfloat16 [128, 128, 32, 256], P(None, 'dom'), may hold values from -0.1875 to 0.1875
- coupling: float32 [128], replicated, may hold values from -1 to 1
- pattern: int32 [8, 2], P('band'), may hold values 0 or 1
Outputs:
- correlation_next: float32 [512, 128], P(('band', 'dom'))
- hamiltonian_next: float32 [512, 128], P(('band', 'dom'))
All inputs are finite; a program needn't handle non-finite values. No bound on the sum of `pattern` on one device may be relied on, other than what follows from the above.
Results may differ from a plain program's by a relative error of at most 0.0033.
The roundings to bfloat16 on the way count: a program that leaves them out, or rounds other values in their place, can miss the bound.
Values may be sent and summed in bfloat16 or wider, within the bound.
A program may use at most 384 MiB of HBM per device.

v0:
```python
import functools

import jax
import jax.numpy as jnp
from jax import lax
from jax.experimental import pallas as pl
from jax.experimental.pallas import tpu as pltpu
from jax.sharding import PartitionSpec as P

W_CENTER = 90.0
W_NEAR = -16.0
W_FAR = 1.0
W_SCALE = 1.0 / 24.0

MESH = pl.DeviceIdType.MESH

HANDED_ON = {0: ((4, False),), 1: ((0, False), (1, True)), 2: ((2, True), (3, False)), 3: ((7, False),)}
CHUNK = 16
PLANES = 4
PARTS = 8


def dot_rows(left, right):
    return lax.dot_general(left, right, (((1,), (1,)), ((), ())), preferred_element_type=jnp.float32)


def kernel(
    orb_hbm, proj_hbm, pot, coupling, pattern, out,
    nat, pnat, pt, ext, far_in, img, other, circ, coef, acc, acc_twin, twin_in,
    rc, s1c, qc, s2c, tc, nb, rr, s1, qq, s2,
    in_sem, pin_sem, halo_s, halo_r, pair_s, pair_r, cross_s, cross_r,
    c1_s, c1_r, c2_s, c2_r, n_s, n_r, f1_s, f1_r, f2_s, f2_r, via_r, via_s, t_s, t_r,
):
    band = lax.axis_index("band")
    dom = lax.axis_index("dom")
    core = lax.rem(band, 2)
    zh = band // 2
    yz = dom // 4
    zl = lax.rem(yz, 2)
    xx = lax.rem(dom, 4)
    partner = zh * 2 + (1 - core)
    cross = (1 - zh) * 2 + (1 - core)
    twin = (1 - zh) * 2 + core
    other_yz = yz + 1 - 2 * lax.rem(yz, 2)
    row_end = (lax.rem(other_yz * 4 + 31, 32), lax.rem(other_yz * 4 + 4, 32))
    is_even = core == 0
    is_odd = core == 1

    def x_peer(j):
        return yz * 4 + lax.rem(xx + j, 4)

    def yz_peer(j):
        return lax.rem(yz + j, 8) * 4 + xx

    def remote(src, dst, ssem, rsem, to_band, to_dom):
        return pltpu.make_async_remote_copy(
            src_ref=src, dst_ref=dst, send_sem=ssem, recv_sem=rsem,
            device_id=(to_band, to_dom), device_id_type=MESH,
        )

    def plane_of(k):
        return lax.rem(k, 2) * 2 + k // 4

    def first_row(k):
        return (1 - lax.rem(k // 2, 2)) * CHUNK

    def rows_of(k):
        return pl.ds(pl.multiple_of(first_row(k), CHUNK), CHUNK)

    def pair_order(i):
        i = lax.rem(i + 4 * (1 - zl), PARTS)
        return lax.rem(3 * (i // 2), 4) + 4 * lax.rem(i, 2)

    def own_order(i):
        return i + core * (pair_order(i) - i)

    def load(src, dst, sem, i):
        k, slot = own_order(i), lax.rem(i, 2)
        return pltpu.make_async_copy(src.at[:, plane_of(k), rows_of(k), :], dst.at[slot], sem.at[slot])

    def own(k):
        return ext.at[plane_of(k) + 2, rows_of(k)]

    def halo(k):
        side = lax.rem(k, 2)
        to_dom = lax.rem(dom + 31 + 2 * side, 32)
        return remote(own(k), ext.at[plane_of(k) + 6 - 8 * side, rows_of(k)], halo_s.at[k], halo_r.at[k], band, to_dom)

    def other_odd(flag, z):
        far = int(flag) + z - 2 * int(flag) * z
        return partner + far * (cross - partner)

    def to_via(k, flag, column):
        dst = ext.at[6 - 6 * (k % 2), pl.ds(0, CHUNK)]
        return remote(own(k), dst, halo_s.at[k], via_r.at[k % 2], other_odd(flag, zl), other_yz * 4 + column)

    def to_twin(k):
        to_dom = lax.rem(dom + 31 + 2 * lax.rem(k, 2), 32)
        return remote(own(k), far_in.at[k // 4], halo_s.at[k], halo_r.at[k], twin, to_dom)

    def via_in(k):
        dst = ext.at[6 - 6 * (k % 2), pl.ds(0, CHUNK)]
        return remote(dst, dst, via_s.at[k % 2], via_r.at[k % 2], partner, row_end[0])

    def via(k, far):
        side = k % 2
        src = ext.at[6 - 6 * side, pl.ds(0, CHUNK)]
        dst = far_in.at[k // 4] if far else ext.at[plane_of(k) + 6 - 8 * side, rows_of(k)]
        return remote(src, dst, via_s.at[side], halo_r.at[k], partner, row_end[side])

    def twin_sum():
        return remote(acc_twin, twin_in, t_s.at[0], t_r.at[0], twin, dom)

    def to_pair(k):
        return remote(own(k), other.at[plane_of(k), rows_of(k), pl.ds(0, 128)], pair_s.at[k], pair_r.at[k], partner, dom)

    def to_cross(k):
        return remote(own(k), other.at[plane_of(k), rows_of(k), pl.ds(128, 128)], cross_s.at[k], cross_r.at[k], cross, dom)

    load(orb_hbm, nat, in_sem, 0).start()
    load(proj_hbm, pnat, pin_sem, 0).start()

    barrier = pltpu.get_barrier_semaphore()
    peers = [(band, x_peer(j)) for j in (1, 2, 3)]
    peers += [(band, yz_peer(j)) for j in range(1, 8)]
    peers += [(partner, dom), (cross, dom)]
    for peer in peers:
        pl.semaphore_signal(barrier, inc=1, device_id=peer, device_id_type=MESH)

    def greet(peer):
        pl.semaphore_signal(barrier, inc=1, device_id=peer, device_id_type=MESH)

    up_end = is_even & (xx == 3)
    down_end = is_even & (xx == 0)
    ahead = lax.rem(yz + 1, 8)
    back = lax.rem(yz + 7, 8)

    for column, chunks in HANDED_ON.items():

        @pl.when(is_odd & (xx == column))
        def _():
            for k, flag in chunks:
                greet((other_odd(flag, 1 - zl), other_yz * 4 + 3 * (k % 2)))
                greet((partner, row_end[k % 2]))

    for end, side, last in ((up_end, 1, ahead), (down_end, 0, back)):

        @pl.when(end)
        def _():
            for b in (band, twin):
                greet((b, lax.rem(dom + 31 + 2 * side, 32)))
            for column, chunks in HANDED_ON.items():
                for k, flag in chunks:
                    if k % 2 == side:
                        greet((other_odd(flag, zl), other_yz * 4 + column))
                    else:
                        greet((partner, (last + 1 - 2 * lax.rem(last, 2)) * 4 + column))

    row = lax.broadcasted_iota(jnp.int32, (256, 256), 0)
    col = lax.broadcasted_iota(jnp.int32, (256, 256), 1)
    gap = (row - col) & 255
    near_z = (gap == 1) | (gap == 255)
    far_z = (gap == 2) | (gap == 254)
    circ[...] = jnp.where(gap == 0, W_CENTER, jnp.where(near_z, W_NEAR, jnp.where(far_z, W_FAR, 0.0))).astype(jnp.bfloat16)
    coef[...] = jnp.zeros_like(coef)
    rc[...] = jnp.zeros_like(rc)

    at_end = up_end | down_end
    def relayout(i):
        load(orb_hbm, nat, in_sem, i).wait()
        slot, k = lax.rem(i, 2), own_order(i)
        px, rows = plane_of(k) + 2, rows_of(k)

        @pl.loop(0, 8)
        def _(q):
            r = pl.ds(pl.multiple_of(q * 16, 16), 16)
            ext[px, rows, r, :] = jnp.swapaxes(nat[slot, r], 0, 1)

    load(orb_hbm, nat, in_sem, 1).start()
    relayout(0)

    edge = (xx == 0) | (xx == 3)
    kinds = (
        (at_end, 8),
        (is_odd & edge, 2),
        (is_odd & jnp.logical_not(edge), 4),
        (is_even & jnp.logical_not(edge), 0),
    )
    for kind, count in kinds:

        @pl.when(kind)
        def _():
            pl.semaphore_wait(barrier, len(peers) + count)

    @pl.loop(0, PARTS)
    def _(i):
        slot = lax.rem(i, 2)
        k = own_order(i)

        @pl.when(i + 1 < PARTS)
        def _():
            load(proj_hbm, pnat, pin_sem, i + 1).start()

        @pl.when((i >= 1) & (i + 1 < PARTS))
        def _():
            load(orb_hbm, nat, in_sem, i + 1).start()

        @pl.when(i >= 1)
        def _():
            relayout(i)

        px = plane_of(k) + 2

        @pl.when(is_even)
        def _():
            for column, chunks in HANDED_ON.items():
                for c, flag in chunks:

                    @pl.when((up_end if c % 2 else down_end) & (k == c))
                    def _():
                        to_via(c, flag, column).start()

            straight = (down_end & (k == 6)) | (up_end & (k == 5))
            across = (down_end & (slot == 0)) | (up_end & (slot == 1))

            @pl.when(straight & (zl == 0))
            def _():
                to_twin(k).start()

            @pl.when(jnp.logical_not(across) | (straight & (zl == 1)))
            def _():
                halo(k).start()

        @pl.when(is_odd)
        def _():
            to_cross(k).start()
            to_pair(k).start()

        load(proj_hbm, pnat, pin_sem, i).wait()

        @pl.loop(0, 8)
        def _(q):
            r = pl.ds(pl.multiple_of(q * 16, 16), 16)
            pt[:, r, :] = jnp.swapaxes(pnat[slot, r], 0, 1)

        first = first_row(k)
        part = coef[...]
        for r in range(CHUNK):
            part = part + dot_rows(pt[r], ext[px, first + r])
        coef[...] = part

    @pl.when(down_end)
    def _():
        ext[0:2, pl.ds(pl.multiple_of(CHUNK * zl, CHUNK), CHUNK), :, :] = jnp.zeros((2, CHUNK, 128, 256), jnp.bfloat16)

    @pl.when(up_end)
    def _():
        ext[6:8, pl.ds(pl.multiple_of(CHUNK * (1 - zl), CHUNK), CHUNK), :, :] = jnp.zeros((2, CHUNK, 128, 256), jnp.bfloat16)

    for d in range(32):
        rc[d % 4, d // 4, 0:4, :] = coef[4 * d:4 * d + 4, :]

    def c1(j):
        return remote(rc.at[lax.rem(xx + j, 4)], s1c.at[j], c1_s.at[j], c1_r.at[j], band, x_peer(j))

    def c2(j):
        return remote(qc.at[lax.rem(yz + j, 8)], s2c.at[j], c2_s.at[j], c2_r.at[j], band, yz_peer(j))

    def n_pair():
        return remote(tc, nb.at[0], n_s.at[0], n_r.at[0], partner, dom)

    def n_cross():
        return remote(tc, nb.at[1], n_s.at[1], n_r.at[1], cross, dom)

    for j in (1, 2, 3):
        c1(j).start()

    def local_rows(start, stop):
        def body(k, carry):
            x = k // 32
            y = lax.rem(k, 32)

            def at(dx, dy):
                return ext[x + 2 + dx, lax.rem(y + 32 + dy, 32)].astype(jnp.float32)

            center = ext[x + 2, y]
            own_z = jnp.dot(center, circ[...], preferred_element_type=jnp.float32)
            near = (at(-1, 0) + at(1, 0)) + (at(0, -1) + at(0, 1))
            far = (at(-2, 0) + at(2, 0)) + (at(0, -2) + at(0, 2))
            kinetic = (own_z + W_NEAR * near + far) * W_SCALE
            img[x, y] = (kinetic + pot[x, pl.ds(y, 1), :] * center.astype(jnp.float32)).astype(jnp.bfloat16)
            return carry

        lax.fori_loop(start, stop, body, 0)

    def first_planes():
        for k in (1, 3, 5, 7):
            halo(k).wait_recv()
        local_rows(0, 64)

    def last_planes():
        for k in (0, 2, 4, 6):
            halo(k).wait_recv()
        local_rows(64, 128)

    @pl.when(down_end)
    def _():
        last_planes()

    @pl.when(is_even & (xx != 0))
    def _():
        first_planes()

    def sum_c1():
        for j in (1, 2, 3):
            c1(j).wait_recv()
        qc[...] = (rc[xx] + s1c[1]) + (s1c[2] + s1c[3])
        for j in range(1, 8):
            c2(j).start()

    def sum_c2():
        for j in range(1, 8):
            c2(j).wait_recv()
        total = qc[yz]
        for j in range(1, 8):
            total = total + s2c[j]
        tc[...] = total

    for column, chunks in HANDED_ON.items():

        for z in range(2):

            @pl.when(is_odd & (xx == column) & (zl == z))
            def _():
                for k, flag in chunks:
                    via_in(k).wait_recv()
                    via(k, flag == (z == 1)).start()

    @pl.when(is_odd)
    def _():
        sum_c1()
        sum_c2()
        n_pair().start()
        n_cross().start()

    def weighted(tile):
        r = lax.broadcasted_iota(jnp.int32, (8, 128), 0)
        scale = jnp.zeros((8, 128), jnp.float32)
        for q in range(4):
            scale = jnp.where(r == q, coupling[4 * dom + q], scale)
        return (scale * tile).astype(jnp.bfloat16).astype(jnp.float32)

    def outer(left, right):
        return lax.dot_general(
            left, right, (((0,), (0,)), ((), ())),
            precision=lax.Precision.HIGHEST, preferred_element_type=jnp.float32,
        )

    def f1(j):
        return remote(rr.at[lax.rem(xx + j, 4)], s1.at[j], f1_s.at[j], f1_r.at[j], band, x_peer(j))

    def f2_own(j):
        return remote(qq.at[0, lax.rem(yz + j, 8)], s2.at[j], f2_s.at[j], f2_r.at[j], band, yz_peer(j))

    def f2_cross(j):
        return remote(qq.at[1, lax.rem(yz + j, 8)], s2.at[j], f2_s.at[8 + j], f2_r.at[j], cross, yz_peer(j))

    @pl.when(down_end)
    def _():
        first_planes()

    @pl.when(is_even & (xx != 0))
    def _():
        last_planes()

    @pl.when(is_even)
    def _():
        sum_c1()
        acc[...] = jnp.zeros_like(acc)

        def products(i):
            k = pair_order(i)
            to_pair(k).wait_recv()
            to_cross(k).wait_recv()
            x = plane_of(k)
            first = first_row(k)

            @pl.loop(0, CHUNK // 4)
            def _(q):
                part = acc[...]
                for r in range(4):
                    y = first + q * 4 + r
                    left = jnp.concatenate([ext[x + 2, y], img[x, y]], axis=0)
                    part = part + dot_rows(left, other[x, y])
                acc[...] = part

        pl.loop(0, 4)(products)

        def twin_products(first, outer_plane, inner_plane, near_at, far_at):
            acc_twin[...] = jnp.zeros_like(acc_twin)

            @pl.loop(0, CHUNK)
            def _(r):
                near = far_in[near_at, r].astype(jnp.float32)
                far = far_in[far_at, r].astype(jnp.float32)
                outer_part = ((W_NEAR * near + W_FAR * far) * W_SCALE).astype(jnp.bfloat16)
                inner_part = ((W_FAR * W_SCALE) * near).astype(jnp.bfloat16)
                acc_twin[...] += dot_rows(outer_part, other[outer_plane, first + r]) + dot_rows(
                    inner_part, other[inner_plane, first + r]
                )

            twin_sum().start()

        @pl.when(down_end)
        def _():
            twin_products(CHUNK * zl, 0, 1, 1, 0)

        @pl.when(up_end)
        def _():
            twin_products(CHUNK * (1 - zl), 3, 2, 0, 1)

        pl.loop(4, PARTS)(products)

        @pl.when(at_end)
        def _():
            twin_sum().wait_recv()
            acc[128:256, 0:128] += twin_in[:, 128:256]
            acc[128:256, 128:256] += twin_in[:, 0:128]

        sum_c2()
        n_pair().wait_recv()
        n_cross().wait_recv()
        mine = tc[...]
        acc[128:256, 0:128] += outer(mine, weighted(nb[0]))
        acc[128:256, 128:256] += outer(weighted(mine), nb[1])
        acc[0:128, 128:256] = acc[0:128, 128:256].T
        acc[128:256, 128:256] = acc[128:256, 128:256].T
        for d in range(32):
            for half in range(2):
                cols = slice(128 * half, 128 * half + 128)
                rr[d % 4, half, d // 4, 0:4, :] = acc[4 * d:4 * d + 4, cols]
                rr[d % 4, half, d // 4, 4:8, :] = acc[128 + 4 * d:128 + 4 * d + 4, cols]
        for j in (1, 2, 3):
            f1(j).start()
        for j in (1, 2, 3):
            f1(j).wait_recv()
        qq[...] = (rr[xx] + s1[1]) + (s1[2] + s1[3])
        for j in range(8):
            f2_cross(j).start()
        for j in range(1, 8):
            f2_own(j).start()
        for j in range(1, 8):
            f2_own(j).wait_recv()
        s2[0] = qq[0, yz]

    @pl.when(is_odd)
    def _():
        for j in range(8):
            f2_cross(j).wait_recv()

    total = s2[0]
    for j in range(1, 8):
        total = total + s2[j]
    lane = lax.broadcasted_iota(jnp.int32, (8, 128), 1)
    block = dom // 16
    mask = jnp.where(lane < 64, pattern[block, 0], pattern[block, 1]).astype(jnp.float32)
    total = total * mask
    out[...] = total

    for j in (1, 2, 3):
        c1(j).wait_send()
    for j in range(1, 8):
        c2(j).wait_send()

    @pl.when(is_even)
    def _():
        for k in range(PARTS):
            halo(k).wait_send()
        for j in (1, 2, 3):
            f1(j).wait_send()
        for j in range(8):
            f2_cross(j).wait_send()
        for j in range(1, 8):
            f2_own(j).wait_send()

    @pl.when(is_odd)
    def _():
        for k in range(PARTS):
            to_pair(k).wait_send()
            to_cross(k).wait_send()
        n_pair().wait_send()
        n_cross().wait_send()

    for column, chunks in HANDED_ON.items():

        @pl.when(is_odd & (xx == column))
        def _():
            for k, _flag in chunks:
                via(k, False).wait_send()

    @pl.when(at_end)
    def _():
        twin_sum().wait_send()


def on_device(orbitals, potential, projectors, coupling, pattern):
    f32, bf16 = jnp.float32, jnp.bfloat16
    dma = lambda n: pltpu.SemaphoreType.DMA((n,))
    hbm = pl.BlockSpec(memory_space=pl.ANY)
    vmem = pl.BlockSpec(memory_space=pltpu.VMEM)
    smem = pl.BlockSpec(memory_space=pltpu.SMEM)
    total = pl.pallas_call(
        kernel,
        out_shape=jax.ShapeDtypeStruct((8, 128), f32),
        in_specs=[hbm, hbm, vmem, smem, smem],
        out_specs=vmem,
        scratch_shapes=[
            pltpu.VMEM((2, 128, CHUNK, 256), bf16),
            pltpu.VMEM((2, 128, CHUNK, 256), bf16),
            pltpu.VMEM((CHUNK, 128, 256), bf16),
            pltpu.VMEM((PLANES + 4, 32, 128, 256), bf16),
            pltpu.VMEM((2, CHUNK, 128, 256), bf16),
            pltpu.VMEM((PLANES, 32, 128, 256), bf16),
            pltpu.VMEM((PLANES, 32, 256, 256), bf16),
            pltpu.VMEM((256, 256), bf16),
            pltpu.VMEM((128, 128), f32),
            pltpu.VMEM((256, 256), f32),
            pltpu.VMEM((128, 256), f32),
            pltpu.VMEM((128, 256), f32),
            pltpu.VMEM((4, 8, 8, 128), f32),
            pltpu.VMEM((4, 8, 8, 128), f32),
            pltpu.VMEM((8, 8, 128), f32),
            pltpu.VMEM((8, 8, 128), f32),
            pltpu.VMEM((8, 128), f32),
            pltpu.VMEM((2, 8, 128), f32),
            pltpu.VMEM((4, 2, 8, 8, 128), f32),
            pltpu.VMEM((4, 2, 8, 8, 128), f32),
            pltpu.VMEM((2, 8, 8, 128), f32),
            pltpu.VMEM((8, 8, 128), f32),
            dma(2), dma(2), dma(8), dma(8), dma(8), dma(8), dma(8), dma(8),
            dma(4), dma(4), dma(8), dma(8), dma(2), dma(2), dma(4), dma(4), dma(16), dma(8), dma(2), dma(2), dma(1), dma(1),
        ],
        compiler_params=pltpu.CompilerParams(
            collective_id=0, has_side_effects=True, vmem_limit_bytes=58 * 2**20,
        ),
    )(orbitals, projectors, potential, coupling, pattern)
    return total[0:4], total[4:8]


def solution(mesh):
    return jax.shard_map(
        on_device,
        mesh=mesh,
        in_specs=(
            P("band", "dom", None, None),
            P("dom", None, None),
            P(None, "dom", None, None),
            P(),
            P("band", None),
        ),
        out_specs=(P(("band", "dom"), None), P(("band", "dom"), None)),
        check_vma=False,
    )
```

profile of v0, /device:TPU:1, one launch (start us, length us, event | category | flops | bytes accessed | tf_op | source)
XLA Modules:
  0.0 130.3 jit_solution(6389871565341250036)
XLA Ops:
  0.6 128.3 %shard_map.68 = f32[8,128]{1,0:T(8,128)} custom-call(bf16[128,4,32,256]{3,2,1,0:T(8,128)(2,1)} %orb_hbm.1, bf16[128,4,32,256]{3,2,1,0:T(8,128)(2,1)} %proj_hbm.1, f32[4,32,256]{2,1,0:T(8,128)} %pot.1, f32[128]{0:T(128)} %coupling.1, s32[2,2]{1,0:T(2,128)} %pattern.1), custom_call_target="tpu_custom_call" | custom-call | tf_op jit(solution)/shard_map/pallas_call | solution.py:512
  129.0 1.3 %fusion = (f32[4,128]{1,0:T(4,128)}, f32[4,128]{1,0:T(4,128)}) fusion(f32[8,128]{1,0:T(8,128)} %shard_map.68), kind=kLoop, calls=%fused_computation | loop fusion | bytes 8192 | tf_op jit(solution)/shard_map/slice | solution.py:547
where the time goes:
time: 131 us; the launch traced here: 130 us
  Pallas kernels  128 us (98%)
  local copies, waits for them, and re-layouts  1.33 us (1%)
    pallas_call x1, Pallas kernels, on_device(): pl.pallas_call(kernel, out_shape=jax.ShapeDtypeStruct((8, 128), f32), in_...  128 us

commit v1 on v0

--- a/solution.py
+++ b/solution.py
@@ -25,11 +25,11 @@
 
 
 def kernel(
-    orb_hbm, proj_hbm, pot, coupling, pattern, out,
-    nat, pnat, pt, ext, far_in, img, other, circ, coef, acc, acc_twin, twin_in,
+    orb_hbm, proj_hbm, pot_hbm, coupling, pattern, out,
+    pot, nat, pnat, pt, ext, far_in, img, other, circ, coef, acc, acc_twin, twin_in,
     rc, s1c, qc, s2c, tc, nb, rr, s1, qq, s2,
     in_sem, pin_sem, halo_s, halo_r, pair_s, pair_r, cross_s, cross_r,
-    c1_s, c1_r, c2_s, c2_r, n_s, n_r, f1_s, f1_r, f2_s, f2_r, via_r, via_s, t_s, t_r,
+    c1_s, c1_r, c2_s, c2_r, n_s, n_r, f1_s, f1_r, f2_s, f2_r, via_r, via_s, t_s, t_r, pot_sem,
 ):
     band = lax.axis_index("band")
     dom = lax.axis_index("dom")
@@ -119,6 +119,7 @@
 
     load(orb_hbm, nat, in_sem, 0).start()
     load(proj_hbm, pnat, pin_sem, 0).start()
+    pltpu.make_async_copy(pot_hbm, pot, pot_sem.at[0]).start()
 
     barrier = pltpu.get_barrier_semaphore()
     peers = [(band, x_peer(j)) for j in (1, 2, 3)]
@@ -257,6 +258,8 @@
     def _():
         ext[6:8, pl.ds(pl.multiple_of(CHUNK * (1 - zl), CHUNK), CHUNK), :, :] = jnp.zeros((2, CHUNK, 128, 256), jnp.bfloat16)
 
+    pltpu.make_async_copy(pot_hbm, pot, pot_sem.at[0]).wait()
+
     for d in range(32):
         rc[d % 4, d // 4, 0:4, :] = coef[4 * d:4 * d + 4, :]
 
@@ -356,8 +359,9 @@
             precision=lax.Precision.HIGHEST, preferred_element_type=jnp.float32,
         )
 
-    def f1(j):
-        return remote(rr.at[lax.rem(xx + j, 4)], s1.at[j], f1_s.at[j], f1_r.at[j], band, x_peer(j))
+    def f1(half, j):
+        src = rr.at[lax.rem(xx + j, 4), half]
+        return remote(src, s1.at[j, half], f1_s.at[4 * half + j], f1_r.at[4 * half + j], band, x_peer(j))
 
     def f2_own(j):
         return remote(qq.at[0, lax.rem(yz + j, 8)], s2.at[j], f2_s.at[j], f2_r.at[j], band, yz_peer(j))
@@ -433,22 +437,24 @@
         mine = tc[...]
         acc[128:256, 0:128] += outer(mine, weighted(nb[0]))
         acc[128:256, 128:256] += outer(weighted(mine), nb[1])
-        acc[0:128, 128:256] = acc[0:128, 128:256].T
-        acc[128:256, 128:256] = acc[128:256, 128:256].T
-        for d in range(32):
-            for half in range(2):
-                cols = slice(128 * half, 128 * half + 128)
+        for half in range(2):
+            cols = slice(128 * half, 128 * half + 128)
+            if half:
+                acc[0:128, cols] = acc[0:128, cols].T
+                acc[128:256, cols] = acc[128:256, cols].T
+            for d in range(32):
                 rr[d % 4, half, d // 4, 0:4, :] = acc[4 * d:4 * d + 4, cols]
                 rr[d % 4, half, d // 4, 4:8, :] = acc[128 + 4 * d:128 + 4 * d + 4, cols]
+            for j in (2, 1, 3):
+                f1(half, j).start()
         for j in (1, 2, 3):
-            f1(j).start()
-        for j in (1, 2, 3):
-            f1(j).wait_recv()
+            f1(0, j).wait_recv()
+            f1(1, j).wait_recv()
         qq[...] = (rr[xx] + s1[1]) + (s1[2] + s1[3])
-        for j in range(8):
+        for j in (4, 3, 5, 2, 6, 1, 7, 0):
             f2_cross(j).start()
-        for j in range(1, 8):
-            f2_own(j).start()
+            if j:
+                f2_own(j).start()
         for j in range(1, 8):
             f2_own(j).wait_recv()
         s2[0] = qq[0, yz]
@@ -477,7 +483,8 @@
         for k in range(PARTS):
             halo(k).wait_send()
         for j in (1, 2, 3):
-            f1(j).wait_send()
+            f1(0, j).wait_send()
+            f1(1, j).wait_send()
         for j in range(8):
             f2_cross(j).wait_send()
         for j in range(1, 8):
@@ -512,9 +519,10 @@
     total = pl.pallas_call(
         kernel,
         out_shape=jax.ShapeDtypeStruct((8, 128), f32),
-        in_specs=[hbm, hbm, vmem, smem, smem],
+        in_specs=[hbm, hbm, hbm, smem, smem],
         out_specs=vmem,
         scratch_shapes=[
+            pltpu.VMEM((PLANES, 32, 256), f32),
             pltpu.VMEM((2, 128, CHUNK, 256), bf16),
             pltpu.VMEM((2, 128, CHUNK, 256), bf16),
             pltpu.VMEM((CHUNK, 128, 256), bf16),
@@ -538,7 +546,7 @@
             pltpu.VMEM((2, 8, 8, 128), f32),
             pltpu.VMEM((8, 8, 128), f32),
             dma(2), dma(2), dma(8), dma(8), dma(8), dma(8), dma(8), dma(8),
-            dma(4), dma(4), dma(8), dma(8), dma(2), dma(2), dma(4), dma(4), dma(16), dma(8), dma(2), dma(2), dma(1), dma(1),
+            dma(4), dma(4), dma(8), dma(8), dma(2), dma(2), dma(8), dma(8), dma(16), dma(8), dma(2), dma(2), dma(1), dma(1), dma(1),
         ],
         compiler_params=pltpu.CompilerParams(
             collective_id=0, has_side_effects=True, vmem_limit_bytes=58 * 2**20,

time: 131 us -> 131 us (level)
  no operation moved by 1% of the time
where the time goes in v1:
time: 131 us; the launch traced here: 130 us
  Pallas kernels  128 us (98%)
  local copies, waits for them, and re-layouts  1.33 us (1%)
    pallas_call x1, Pallas kernels, on_device(): pl.pallas_call(kernel, out_shape=jax.ShapeDtypeStruct((8, 128), f32), in_...  128 us

profile of v1, /device:TPU:1, one launch (start us, length us, event | category | flops | bytes accessed | tf_op | source)
XLA Modules:
  0.0 130.2 jit_solution(2830305876822383300)
XLA Ops:
  0.6 128.2 %shard_map.68 = f32[8,128]{1,0:T(8,128)} custom-call(bf16[128,4,32,256]{3,2,1,0:T(8,128)(2,1)} %orb_hbm.1, bf16[128,4,32,256]{3,2,1,0:T(8,128)(2,1)} %proj_hbm.1, f32[4,32,256]{2,1,0:T(8,128)} %pot_hbm.1, f32[128]{0:T(128)} %coupling.1, s32[2,2]{1,0:T(2,128)} %pattern.1), custom_call_target="tpu_custom_call" | custom-call | tf_op jit(solution)/shard_map/pallas_call | solution.py:519
  128.8 1.3 %fusion = (f32[4,128]{1,0:T(4,128)}, f32[4,128]{1,0:T(4,128)}) fusion(f32[8,128]{1,0:T(8,128)} %shard_map.68), kind=kLoop, calls=%fused_computation | loop fusion | bytes 8192 | tf_op jit(solution)/shard_map/slice | solution.py:555
